TPU v7x, 256 devices: a whole 4x4x8 slice. The times are simulated.
256 devices in a mesh: dp: 8 (over z), pack: 32 (over x, y, core).
Axes of the slice: x: 4, y: 4, z: 8, core: 2. Of those that a mesh axis runs over, the one named last changes fastest.
Arguments:
- enc_keys: bfloat16 [65536, 4096], P(('dp', 'pack')), may hold values from -4 to 4
- enc_values: bfloat16 [65536, 4096], P(('dp', 'pack')), may hold values from -6 to 6
- dec_queries: bfloat16 [32768, 4096], P(('dp', 'pack')), may hold values from -4 to 4
- cotangent: bfloat16 [32768, 4096], P(('dp', 'pack')), may hold values from -6 to 6
- input_lengths: int32 [8, 64], P('dp'), may hold values from 16 to 240, as said below
- target_lengths: int32 [8, 64], P('dp'), may hold values from 8 to 120, as said below
- enc_pack: int32 [8, 64], P('dp'), may hold values from 0 to 31, as said below
- dec_pack: int32 [8, 64], P('dp'), may hold values from 0 to 31, as said below
- task_group: int32 [8, 64, 1], P('dp'), may hold values from 0 to 15
- dro_weights: int32 [16], replicated, may hold values from 1 to 8
Outputs:
- queries_gradient: bfloat16 [32768, 4096], P(('dp', 'pack'))
- keys_gradient: bfloat16 [65536, 4096], P(('dp', 'pack'))
- values_gradient: bfloat16 [65536, 4096], P(('dp', 'pack'))
- group_loss: float32 [16], replicated
Inputs may be any that keep to these rules, and one draw needn't show every extreme that they name: `input_lengths`: within one data group, the input lengths of the examples of one encoder pack add up to exactly 256; every length is a multiple of 16. `target_lengths`: within one data group, the target lengths of the examples of one decoder pack add up to exactly 128; every length is a multiple of 8. `enc_pack`: within one data group, every encoder pack holds exactly 2 examples. `dec_pack`: within one data group, every decoder pack holds exactly 2 examples.
All inputs are finite; a program needn't handle non-finite values.
Results may differ from a plain program's by a relative error of at most 0.012.
The roundings to bfloat16 on the way count: a program that leaves them out, or rounds other values in their place, can miss the bound.
Values may be sent and summed in bfloat16 or wider, within the bound.
A program may use at most 128 MiB of HBM per device.

v0:
```python
import jax
import jax.numpy as jnp
from jax import lax
from jax.sharding import PartitionSpec as P

HEAD_DIM = 64
EX_DEV = 2
GROUPS = 16


def owner_value(member, values):
    return jnp.sum(jnp.where(member, values[:, None], 0), axis=0)


def pack_tables(lengths, pack_index, per_pack, slot_total, pack_total):
    ordinal = jnp.arange(lengths.shape[0], dtype=jnp.int32)
    same_pack = pack_index[:, None] == pack_index[None, :]
    earlier = ordinal[None, :] < ordinal[:, None]
    offsets = jnp.sum(jnp.where(same_pack & earlier, lengths[None, :], 0), axis=1)
    places = jnp.arange(slot_total, dtype=jnp.int32)
    inside = places[None, :] < lengths[:, None]
    starts = pack_index * per_pack + offsets
    tokens = jnp.arange(pack_total * per_pack, dtype=jnp.int32)
    token_pack = tokens // per_pack
    token_place = tokens % per_pack
    member = (
        (pack_index[:, None] == token_pack[None, :])
        & (offsets[:, None] <= token_place[None, :])
        & (token_place[None, :] < (offsets + lengths)[:, None])
    )
    return (starts, inside, member)


def padded_table(table, extra):
    return jnp.concatenate([table, jnp.zeros((extra, table.shape[1]), table.dtype)], axis=0)


def take_rows(table, starts, slot_total):
    return jnp.stack(
        [lax.dynamic_slice_in_dim(table, starts[item], slot_total, 0) for item in range(EX_DEV)],
        axis=0,
    )


def put_rows(buffer, block, starts, inside):
    slot_total = block.shape[1]
    for item in range(EX_DEV):
        current = lax.dynamic_slice_in_dim(buffer, starts[item], slot_total, 0)
        merged = jnp.where(inside[item][:, None], block[item], current)
        buffer = lax.dynamic_update_slice_in_dim(buffer, merged, starts[item], 0)
    return buffer


def split_heads(block):
    return block.reshape(block.shape[0], block.shape[1], block.shape[2] // HEAD_DIM, HEAD_DIM)


def merge_heads(block):
    return block.reshape(block.shape[0], block.shape[1], -1)


def probabilities(query_block, key_block, key_inside):
    scores = jnp.einsum(
        "eqhd,ekhd->ehqk",
        split_heads(query_block),
        split_heads(key_block),
        preferred_element_type=jnp.float32,
    )
    scores = jnp.where(key_inside[:, None, None, :], scores, -1e30)
    highest = jnp.max(scores, axis=-1, keepdims=True)
    powers = jnp.exp(scores - highest)
    return powers / jnp.sum(powers, axis=-1, keepdims=True)


def local(
    enc_keys,
    enc_values,
    dec_queries,
    cotangent,
    input_lengths,
    target_lengths,
    enc_pack,
    dec_pack,
    task_group,
    dro_weights,
):
    pack_total = lax.axis_size("pack")
    own_pack = lax.axis_index("pack")
    encoder_rows = enc_keys.shape[0]
    decoder_rows = dec_queries.shape[0]
    encoder_slot = 2 * encoder_rows // EX_DEV - 16
    decoder_slot = 2 * decoder_rows // EX_DEV - 8
    encoder_lengths = input_lengths[0]
    decoder_lengths = target_lengths[0]
    encoder_packs = enc_pack[0]
    decoder_packs = dec_pack[0]
    task_row = task_group[0, :, 0]
    group_index = jnp.arange(GROUPS, dtype=jnp.int32)
    group_match = task_row[:, None] == group_index[None, :]
    key_starts, key_inside, key_member = pack_tables(
        encoder_lengths, encoder_packs, encoder_rows, encoder_slot, pack_total
    )
    query_starts, query_inside, query_member = pack_tables(
        decoder_lengths, decoder_packs, decoder_rows, decoder_slot, pack_total
    )
    token_group = owner_value(query_member, task_row)
    group_counts = jnp.sum(jnp.where(group_match, decoder_lengths[:, None], 0), axis=0).astype(
        jnp.float32
    )
    counts = lax.psum(group_counts, "dp")
    key_heads, value_heads = (
        lax.all_to_all(enc_keys, "pack", split_axis=1, concat_axis=0, tiled=True),
        lax.all_to_all(enc_values, "pack", split_axis=1, concat_axis=0, tiled=True),
    )
    query_heads = lax.all_to_all(dec_queries, "pack", split_axis=1, concat_axis=0, tiled=True)
    head_width = key_heads.shape[1]
    query_group_rows = query_heads.shape[0]
    key_group_rows = key_heads.shape[0]
    key_table = padded_table(key_heads, encoder_slot)
    query_table = padded_table(query_heads, decoder_slot)
    query_start_blocks = query_starts.reshape(-1, EX_DEV)
    key_start_blocks = key_starts.reshape(-1, EX_DEV)
    key_inside_blocks = key_inside.reshape(-1, EX_DEV, encoder_slot)
    query_inside_blocks = query_inside.reshape(-1, EX_DEV, decoder_slot)

    def forward_block(entries):
        starts_query, starts_key, inside_key = entries
        return probabilities(
            take_rows(query_table, starts_query, decoder_slot),
            take_rows(key_table, starts_key, encoder_slot),
            inside_key,
        ).astype(jnp.bfloat16)

    attention_store = lax.map(
        forward_block, (query_start_blocks, key_start_blocks, key_inside_blocks)
    )
    value_table = padded_table(value_heads, encoder_slot)

    def output_step(buffer, entries):
        attention_low, starts_key, starts_query, inside_query = entries
        value_block = take_rows(value_table, starts_key, encoder_slot)
        attended = jnp.einsum(
            "ehqk,ekhd->eqhd",
            attention_low,
            split_heads(value_block),
            preferred_element_type=jnp.float32,
        )
        block = merge_heads(attended.astype(jnp.bfloat16))
        return (put_rows(buffer, block, starts_query, inside_query), block)

    attended_start = jnp.zeros((query_group_rows + decoder_slot, head_width), jnp.bfloat16)
    attended_buffer, attended_store = lax.scan(
        output_step,
        attended_start,
        (attention_store, key_start_blocks, query_start_blocks, query_inside_blocks),
    )
    attended_heads = attended_buffer[:query_group_rows]
    total_tokens = decoder_rows * pack_total * lax.axis_size("dp")
    attended_tokens = lax.all_to_all(
        attended_heads, "pack", split_axis=0, concat_axis=1, tiled=True
    )
    token_loss = jnp.sum(
        attended_tokens.astype(jnp.float32) * cotangent.astype(jnp.float32), axis=1
    )
    loss_group = lax.dynamic_slice_in_dim(token_group, own_pack * decoder_rows, decoder_rows)
    loss_part = jnp.sum(
        jnp.where(loss_group[None, :] == group_index[:, None], token_loss[None, :], 0.0), axis=1
    )
    loss_sum = lax.psum(loss_part, ("dp", "pack"))
    group_loss = loss_sum / counts
    weights = dro_weights.astype(jnp.float32)
    scales = weights / jnp.sum(weights) * (total_tokens / counts)
    example_scale = jnp.sum(jnp.where(group_match, scales[None, :], 0.0), axis=1)
    token_scale = owner_value(query_member, example_scale)
    own_scale = lax.dynamic_slice_in_dim(token_scale, own_pack * decoder_rows, decoder_rows)
    upstream = (cotangent.astype(jnp.float32) * own_scale[:, None]).astype(jnp.bfloat16)
    upstream_heads = lax.all_to_all(upstream, "pack", split_axis=1, concat_axis=0, tiled=True)
    upstream_table = padded_table(upstream_heads, decoder_slot)

    def backward_step(buffers, entries):
        query_buffer, key_buffer, value_buffer = buffers
        starts_query, starts_key, inside_key, inside_query, attention_low, attended = entries
        query_block = take_rows(query_table, starts_query, decoder_slot)
        key_block = take_rows(key_table, starts_key, encoder_slot)
        value_split = split_heads(take_rows(value_table, starts_key, encoder_slot))
        gradient = jnp.where(
            inside_query[:, :, None],
            take_rows(upstream_table, starts_query, decoder_slot),
            jnp.zeros((), jnp.bfloat16),
        )
        gradient_split = split_heads(gradient)
        attention = probabilities(query_block, key_block, inside_key)
        value_gradient = jnp.einsum(
            "ehqk,eqhd->ekhd", attention_low, gradient_split, preferred_element_type=jnp.float32
        ).astype(jnp.bfloat16)
        attention_gradient = jnp.einsum(
            "eqhd,ekhd->ehqk", gradient_split, value_split, preferred_element_type=jnp.float32
        )
        row_drift = jnp.einsum(
            "eqhd,eqhd->ehq",
            gradient_split,
            split_heads(attended),
            preferred_element_type=jnp.float32,
        )
        scores_gradient = (attention * (attention_gradient - row_drift[:, :, :, None])).astype(
            jnp.bfloat16
        )
        query_gradient = jnp.einsum(
            "ehqk,ekhd->eqhd",
            scores_gradient,
            split_heads(key_block),
            preferred_element_type=jnp.float32,
        ).astype(jnp.bfloat16)
        key_gradient = jnp.einsum(
            "ehqk,eqhd->ekhd",
            scores_gradient,
            split_heads(query_block),
            preferred_element_type=jnp.float32,
        ).astype(jnp.bfloat16)
        query_buffer = put_rows(
            query_buffer, merge_heads(query_gradient), starts_query, inside_query
        )
        key_buffer = put_rows(key_buffer, merge_heads(key_gradient), starts_key, inside_key)
        value_buffer = put_rows(value_buffer, merge_heads(value_gradient), starts_key, inside_key)
        return ((query_buffer, key_buffer, value_buffer), None)

    starting = (
        jnp.zeros((query_group_rows + decoder_slot, head_width), jnp.bfloat16),
        jnp.zeros((key_group_rows + encoder_slot, head_width), jnp.bfloat16),
        jnp.zeros((key_group_rows + encoder_slot, head_width), jnp.bfloat16),
    )
    finished, unused = lax.scan(
        backward_step,
        starting,
        (
            query_start_blocks,
            key_start_blocks,
            key_inside_blocks,
            query_inside_blocks,
            attention_store,
            attended_store,
        ),
    )
    query_result = finished[0][:query_group_rows]
    key_result = finished[1][:key_group_rows]
    value_result = finished[2][:key_group_rows]
    queries_gradient = lax.all_to_all(query_result, "pack", split_axis=0, concat_axis=1, tiled=True)
    keys_gradient, values_gradient = (
        lax.all_to_all(key_result, "pack", split_axis=0, concat_axis=1, tiled=True),
        lax.all_to_all(value_result, "pack", split_axis=0, concat_axis=1, tiled=True),
    )
    return (queries_gradient, keys_gradient, values_gradient, group_loss)


def solution(mesh):
    placed = (
        P(("dp", "pack"), None),
        P(("dp", "pack"), None),
        P(("dp", "pack"), None),
        P(("dp", "pack"), None),
        P("dp", None),
        P("dp", None),
        P("dp", None),
        P("dp", None),
        P("dp", None, None),
        P(),
    )
    return jax.shard_map(
        local,
        mesh=mesh,
        in_specs=placed,
        out_specs=(P(("dp", "pack"), None), P(("dp", "pack"), None), P(("dp", "pack"), None), P()),
        check_vma=False,
    )
```

profile of v0, /device:TPU:1, one launch (start us, length us, event | category | flops | bytes accessed | tf_op | source)
XLA Modules:
  0.0 2003.8 jit_solution(5040121211303394095)
XLA Ops:
  3.1 8.6 all-to-all-start.1
  14.1 14.4 all-to-all-done.1
  28.6 4.1 all-to-all-start
  35.8 4.1 copy.96
  43.9 17.1 all-to-all-done
  62.3 4.5 all-to-all-start.3
  66.8 4.1 copy.91
  70.9 4.1 copy.130
  78.1 386.8 %while.36 = (s32[]{:T(128)}, bf16[32,2,2,120,240]{4,3,2,1,0:T(8,128)(2,1)}, pred[32,2,240]{2,1,0:T(4,128)(4,1)S(1)}, s32[32,2]{0,1:T(2,128)S(1)}, bf16[4216,128]...) while((s32[]{:T(128)}, ...), condition=%wide.region_5.6_spmd, body=%wide.region_2.5_spmd.sunk | while | flops 15300012 | bytes 801005 | solution.py:134
  472.2 405.4 %while.37 = (s32[]{:T(128)}, bf16[4216,128]{0,1:T(8,128)(2,1)S(1)}, bf16[32,2,120,128]{2,3,1,0:T(8,128)(2,1)}, pred[32,2,120]{2,1,0:T(4,128)(4,1)S(1)}, s32[32,2...) while((s32[]{:T(128)}, bf16[4216,128]{0,1:T(8,128)(2,1)S(1)}, ...), condition=%wide.region_7.8_spmd, body=%wide.region_6.7_spmd.sunk | while | flops 14868494 | bytes 1235469 | solution.py:152
  880.3 7.5 all-to-all-start.7
  887.9 17.1 psum.14
  913.3 10.3 all-to-all-start.2
  923.5 16.9 all-to-all-done.2
  945.5 885.5 %while.38 = (s32[]{:T(128)}, bf16[4216,128]{0,1:T(8,128)(2,1)}, bf16[8432,128]{0,1:T(8,128)(2,1)S(1)}, bf16[8432,128]{0,1:T(8,128)(2,1)}, pred[32,2,120]{2,1,0:T...) while((s32[]{:T(128)}, bf16[4216,128]{0,1:T(8,128)(2,1)}, ...), condition=%wide.region_16.17_spmd, body=%wide.region_13.16_spmd.sunk | while | flops 75394336 | bytes 5927545 | solution.py:232
  1843.1 11.3 all-to-all-done.4
  1854.4 4.7 all-to-all-start.5
  1860.7 4.1 copy.115
  1864.7 22.7 %all-to-all-done.5 = bf16[32,256,128]{2,1,0:T(8,128)(2,1)} async-done(((bf16[32,256,128]{2,1,0:T(8,128)(2,1)}), bf16[32,256,128]{2,1,0:T(8,128)(2,1)}, u32[]{:S(2)}, u32[]{:S(2)}) %all-to-all-start.5) | async-done | bytes 2097184 | tf_op jit(solution)/shard_map/all_to_all | solution.py:249
  1887.5 4.5 all-to-all-start.6
  1892.6 92.0 %psum.15 = f32[16]{0:T(128)S(1)} all-reduce(f32[16]{0:T(128)S(1)} %select_reduce_fusion.4), channel_id=1, replica_groups=mesh['dp'=8,'pack'=32] {'dp','pack'}, use_global_device_ids=true, to_apply=%region_20.21 | all-reduce | flops 16 | bytes 128 | tf_op jit(solution)/shard_map/psum | solution.py:169
  1988.7 4.1 copy.114
  1992.7 4.1 copy.121
  1999.7 4.1 copy.122
  (1718 shorter events, 1005.5 us)
Async XLA Ops:
  0.6 11.0 copy-start.2
  3.1 25.5 %all-to-all-start.1 = ((bf16[128,32,128]{0,2,1:T(8,128)(2,1)}), bf16[128,32,128]{0,2,1:T(8,128)(2,1)S(1)}, u32[]{:S(2)}, u32[]{:S(2)}) async-start(bf16[128,32,128]{0,2,1:T(8,128)(2,1)} %bitcast.60), calls=%async_computation.1 | async-start | bytes 2097152 | tf_op jit(solution)/shard_map/all_to_all | solution.py:115
  28.6 4.1 copy-start.3
  28.6 4.1 copy-start.8
  28.6 4.4 copy-start.4
  28.6 6.0 copy-start.6
  28.6 32.4 %all-to-all-start = ((bf16[256,32,128]{0,2,1:T(8,128)(2,1)}), bf16[256,32,128]{0,2,1:T(8,128)(2,1)S(1)}, u32[]{:S(2)}, u32[]{:S(2)}) async-start(bf16[256,32,128]{0,2,1:T(8,128)(2,1)} %bitcast.216), calls=%async_computation | async-start | bytes 4194304 | tf_op jit(solution)/shard_map/all_to_all | solution.py:112
  61.0 1.3 copy-start.1
  62.3 402.6 %all-to-all-start.3 = ((bf16[256,32,128]{0,2,1:T(8,128)(2,1)}), bf16[256,32,128]{0,2,1:T(8,128)(2,1)S(1)}, u32[]{:S(2)}, u32[]{:S(2)}) async-start(bf16[256,32,128]{0,2,1:T(8,128)(2,1)} %bitcast.67), calls=%async_computation.3 | async-start | bytes 4194304 | tf_op jit(solution)/shard_map/all_to_all | solution.py:113
  879.0 8.8 copy-start.5
  879.0 26.1 %copy-start.7 = (s32[16]{0:T(128)S(1)}, s32[16]{0:T(128)}, u32[]{:S(2)}) copy-start(s32[16]{0:T(128)} %param.25) | copy-start | bytes 196
  880.3 26.5 %all-to-all-start.7 = ((bf16[32,128,128]{1,2,0:T(8,128)(2,1)}), bf16[32,128,128]{1,2,0:T(8,128)(2,1)S(1)}, u32[]{:S(2)}, u32[]{:S(2)}) async-start(bf16[32,128,128]{1,2,0:T(8,128)(2,1)} %copy.118), calls=%async_computation.7 | async-start | bytes 2097152 | tf_op jit(solution)/shard_map/all_to_all | solution.py:159
  913.3 27.2 %all-to-all-start.2 = ((bf16[128,32,128]{0,2,1:T(8,128)(2,1)}), bf16[128,32,128]{0,2,1:T(8,128)(2,1)S(1)}, u32[]{:S(2)}, u32[]{:S(2)}) async-start(bf16[128,32,128]{0,2,1:T(8,128)(2,1)} %bitcast.64), calls=%async_computation.2 | async-start | bytes 2097152 | tf_op jit(solution)/shard_map/all_to_all | solution.py:177
  1833.6 20.9 %all-to-all-start.4 = ((bf16[32,128,128]{2,1,0:T(8,128)(2,1)}), bf16[32,128,128]{2,1,0:T(8,128)(2,1)S(1)}, u32[]{:S(2)}, u32[]{:S(2)}) async-start(bf16[32,128,128]{2,1,0:T(8,128)(2,1)} %bitcast.236), calls=%async_computation.4 | async-start | bytes 2097152 | tf_op jit(solution)/shard_map/all_to_all | solution.py:247
  1854.4 4.7 copy-start
  1854.4 33.0 %all-to-all-start.5 = ((bf16[32,256,128]{2,1,0:T(8,128)(2,1)}), bf16[32,256,128]{2,1,0:T(8,128)(2,1)}, u32[]{:S(2)}, u32[]{:S(2)}) async-start(bf16[32,256,128]{2,1,0:T(8,128)(2,1)} %bitcast.217), calls=%async_computation.5 | async-start | bytes 4194304 | tf_op jit(solution)/shard_map/all_to_all | solution.py:249
  1887.5 109.3 %all-to-all-start.6 = ((bf16[32,256,128]{2,1,0:T(8,128)(2,1)}), bf16[32,256,128]{2,1,0:T(8,128)(2,1)S(1)}, u32[]{:S(2)}, u32[]{:S(2)}) async-start(bf16[32,256,128]{2,1,0:T(8,128)(2,1)} %bitcast.76), calls=%async_computation.6 | async-start | bytes 4194304 | tf_op jit(solution)/shard_map/all_to_all | solution.py:250
where the time goes:
time: 2040 us; the launch traced here: 2000 us
  loops' own time  733 us (36%)
  local copies, waits for them, and re-layouts  689 us (34%)
  matrix products  201 us (10%)
  other arithmetic  140 us (7%)
  blocking collectives  109 us (5%)
  waiting for transfers between devices  82.5 us (4%)
  starting transfers between devices  48.1 us (2%)
    dynamic_update_slice x256, local copies, waits for them, and re-layouts, put_rows(): buffer = lax.dynamic_update_slice_in_dim(buffer, merged, starts[item], 0)  281 us
    another operation x1, loops' own time, local(): lax.scan(output_step, attended_start, (attention_store, key_start_blocks,...  250 us
    another operation x1, loops' own time, local(): lax.map(forward_block, (query_start_blocks, key_start_blocks, key_inside_...  249 us
    another operation x1, loops' own time, local(): lax.scan(backward_step, starting, (query_start_blocks, key_start_blocks,...  234 us
    dynamic_slice x160, local copies, waits for them, and re-layouts, take_rows(): lax.dynamic_slice_in_dim(table, starts[item], slot_total, 0)  171 us
    select_n x192, other arithmetic, put_rows(): merged = jnp.where(inside[item][:, None], block[item], current)  131 us
    psum x1, blocking collectives, local(): loss_sum = lax.psum(loss_part, ('dp', 'pack'))  92 us
    slice x160, local copies, waits for them, and re-layouts, take_rows(): starts[item]  82.9 us
  transfers between devices with their start and end apart: 8, of which 5 were waited for; matrix products, arithmetic and copies ran while one was open for 9% of the time, Pallas kernels for 0%

commit v1 on v0

v1 whole, which is shorter than its diff:
```python
import functools

import jax
import jax.numpy as jnp
from jax import lax
from jax.experimental import pallas as pl
from jax.experimental.pallas import tpu as pltpu
from jax.sharding import PartitionSpec as P

HEAD_DIM = 64
GROUPS = 16
NP = 32
SLOT = 15
PAIR = 2 * SLOT
TABLE = NP * 16
MESH = pl.DeviceIdType.MESH


def kernel(
    qstart, eslot, first, mine, scale,
    k_hbm, v_hbm, q_hbm, c_hbm,
    dq_out, dk_out, dv_out, loss_out,
    kv, vv, qt, ct, sq, sc, qin, cin, sd, bq, dp, dks, dvs,
    lsem, s1q, r1q, s1c, r1c, s2q, r2q, s2c, r2c, s3, r3, s4, r4, ksem, vsem,
):
    me = lax.axis_index("pack")

    def peer(k):
        return lax.rem(me + k, NP)

    def back(k):
        return lax.rem(me - k + NP, NP)

    def cols(i):
        return pl.ds(pl.multiple_of(i * 128, 128), 128)

    load_k = pltpu.make_async_copy(k_hbm, kv, lsem.at[0])
    load_v = pltpu.make_async_copy(v_hbm, vv, lsem.at[1])

    barrier = pltpu.get_barrier_semaphore()

    def greet(k, carry):
        pl.semaphore_signal(barrier, inc=1, device_id={"pack": peer(k)}, device_id_type=MESH)
        return carry

    lax.fori_loop(1, NP, greet, 0)
    pl.semaphore_wait(barrier, NP - 1)

    def spread(src, dst, send, recv):
        def make(k):
            return pltpu.make_async_remote_copy(
                src_ref=src.at[:, :, cols(peer(k))],
                dst_ref=dst.at[pl.ds(me * 16, 16)],
                send_sem=send.at[k],
                recv_sem=recv.at[k],
                device_id={"pack": peer(k)},
                device_id_type=MESH,
            )
        return make

    def run(count_from, body):
        def step(k, carry):
            body(k)
            return carry
        lax.fori_loop(count_from, NP, step, 0)

    q1 = spread(q_hbm, qt, s1q, r1q)
    c1 = spread(c_hbm, ct, s1c, r1c)
    own_q = pltpu.make_async_copy(q_hbm.at[:, :, cols(me)], qt.at[pl.ds(me * 16, 16)], lsem.at[2])
    own_c = pltpu.make_async_copy(c_hbm.at[:, :, cols(me)], ct.at[pl.ds(me * 16, 16)], lsem.at[3])
    run(1, lambda k: q1(k).start())
    own_q.start()
    run(1, lambda k: c1(k).start())
    own_c.start()
    load_k.start()
    load_v.start()
    qt[pl.ds(TABLE, 16)] = jnp.zeros((16, 8, 128), jnp.bfloat16)
    ct[pl.ds(TABLE, 16)] = jnp.zeros((16, 8, 128), jnp.bfloat16)

    def deal(table, send_buf, into, send, recv):
        def make(k):
            return pltpu.make_async_remote_copy(
                src_ref=send_buf.at[k],
                dst_ref=into.at[k],
                send_sem=send.at[k],
                recv_sem=recv.at[k],
                device_id={"pack": peer(k)},
                device_id_type=MESH,
            )

        def fill(k, dst):
            p = peer(k)
            for a in range(2):
                start = qstart[2 * p + a]
                dst[k, pl.ds(a * SLOT, SLOT)] = table[pl.ds(start, SLOT)]

        return make, fill

    q2, fill_q = deal(qt, sq, qin, s2q, r2q)
    c2, fill_c = deal(ct, sc, cin, s2c, r2c)

    def arrived_1(make, i):
        make(i).wait_recv()

    run(1, lambda k: q1(k).wait_recv())
    own_q.wait()

    def send_q(k):
        fill_q(k, sq)
        q2(k).start()

    run(1, send_q)
    fill_q(0, qin)

    run(1, lambda k: c1(k).wait_recv())
    own_c.wait()

    def send_c(k):
        fill_c(k, sc)
        c2(k).start()

    run(1, send_c)
    fill_c(0, cin)
    load_k.wait()
    load_v.wait()

    len0 = mine[0]
    len1 = mine[1]
    keys0 = mine[2]
    scale0 = scale[0]
    scale1 = scale[1]
    place_c = lax.broadcasted_iota(jnp.int32, (256, 1), 0)
    place_r = lax.broadcasted_iota(jnp.int32, (1, 256), 1)

    def valid_of(place):
        return jnp.where(place < 120, place < len0, place - 120 < len1)

    scale_c = jnp.where(place_c < 120, scale0, scale1)
    scale_r = jnp.where(place_r < 120, scale0, scale1)
    live_c = jnp.where(place_c < 120, jnp.where(place_c < len0, 1.0, 0.0), jnp.where(place_c - 120 < len1, 1.0, 0.0))
    live_r = jnp.where(place_r < 120, jnp.where(place_r < len0, 1.0, 0.0), jnp.where(place_r - 120 < len1, 1.0, 0.0))
    live_c2 = jnp.broadcast_to(live_c, (256, 128)) > 0.5
    live_r2 = jnp.broadcast_to(live_r, (128, 256)) > 0.5
    lane = lax.broadcasted_iota(jnp.int32, (256, 128), 1)
    key_place = lax.broadcasted_iota(jnp.int32, (256, 256), 0)
    query_place = lax.broadcasted_iota(jnp.int32, (256, 256), 1)
    bias = jnp.where(
        jnp.where(query_place < 120, key_place, keys0) < jnp.where(query_place < 120, keys0, key_place + 1),
        0.0, -1e30,
    ).astype(jnp.float32)
    nt = (((1,), (1,)), ((), ()))
    nn = (((1,), (0,)), ((), ()))

    def dot(a, b, dims):
        return lax.dot_general(a, b, dims, preferred_element_type=jnp.float32)

    def flat(ref, k):
        block = ref[k].astype(jnp.float32).reshape(240, 128)
        return jnp.concatenate([block, jnp.zeros((16, 128), jnp.float32)], axis=0)

    def d3(k):
        return pltpu.make_async_remote_copy(
            src_ref=sd.at[k],
            dst_ref=bq.at[pl.ds(me * PAIR, PAIR)],
            send_sem=s3.at[k],
            recv_sem=r3.at[k],
            device_id={"pack": back(k)},
            device_id_type=MESH,
        )

    def out_k(k):
        return pltpu.make_async_copy(dks.at[k], dk_out.at[:, cols(back(k))], ksem.at[k])

    def out_v(k):
        return pltpu.make_async_copy(dvs.at[k], dv_out.at[:, cols(back(k))], vsem.at[k])

    def compute(k, loss):
        i = back(k)
        q = flat(qin, k)
        c = flat(cin, k)
        kb = kv[:, cols(i)]
        vb = vv[:, cols(i)]
        k_t = kb.T
        v_t = vb.T
        c_t = c.T
        u = jnp.where(live_c2, (c * scale_c).astype(jnp.bfloat16).astype(jnp.float32), 0.0)
        u_t = jnp.where(live_r2, (c_t * scale_r).astype(jnp.bfloat16).astype(jnp.float32), 0.0)
        dk = jnp.zeros((256, 128), jnp.float32)
        dv = jnp.zeros((256, 128), jnp.float32)
        dq_parts = []
        for h in range(2):
            own = (lane < 64) if h == 0 else (lane >= 64)
            q_h = jnp.where(own, q, 0.0).astype(jnp.bfloat16)
            u_h = jnp.where(own, u, 0.0).astype(jnp.bfloat16)
            scores = dot(kb, q_h, nt) + bias
            highest = jnp.max(scores, axis=0, keepdims=True)
            powers = jnp.exp(scores - highest)
            attention = powers * (1.0 / jnp.sum(powers, axis=0, keepdims=True))
            low = attention.astype(jnp.bfloat16)
            attended = dot(v_t[h * 64:(h + 1) * 64], low, nn).astype(jnp.bfloat16).astype(jnp.float32)
            loss = loss + jnp.sum(attended * c_t[h * 64:(h + 1) * 64], axis=0, keepdims=True)
            drift = jnp.sum(attended * u_t[h * 64:(h + 1) * 64], axis=0, keepdims=True)
            dv = dv + dot(low, u_h, nn)
            grad = dot(vb, u_h, nt)
            ds = (attention * (grad - drift)).astype(jnp.bfloat16)
            dq_parts.append(dot(k_t[h * 64:(h + 1) * 64], ds, nn))
            dk = dk + dot(ds, q_h, nn)
        dq = jnp.concatenate(dq_parts, axis=0).T
        dks[k] = dk.astype(jnp.bfloat16)
        dvs[k] = dv.astype(jnp.bfloat16)
        sd_block = dq[:240].reshape(PAIR, 8, 128).astype(jnp.bfloat16)
        return sd_block, loss

    block, loss = compute(0, jnp.zeros((1, 256), jnp.float32))
    bq[pl.ds(me * PAIR, PAIR)] = block
    out_k(0).start()
    out_v(0).start()

    def pair_step(k, loss):
        q2(k).wait_recv()
        c2(k).wait_recv()
        block, loss = compute(k, loss)
        sd[k] = block
        d3(k).start()
        out_k(k).start()
        out_v(k).start()
        return loss

    loss = lax.fori_loop(1, NP, pair_step, loss)
    loss_out[...] = jnp.where(live_r > 0.5, loss, 0.0)

    run(1, lambda k: d3(k).wait_recv())

    def d4(k):
        return pltpu.make_async_remote_copy(
            src_ref=dp.at[k],
            dst_ref=dq_out.at[:, :, cols(me)],
            send_sem=s4.at[k],
            recv_sem=r4.at[k],
            device_id={"pack": peer(k)},
            device_id_type=MESH,
        )

    own_d = pltpu.make_async_copy(dp.at[0], dq_out.at[:, :, cols(me)], lsem.at[4])

    def fill_d(k):
        d = peer(k)
        near = eslot[2 * d] * SLOT
        count = first[d]
        far = eslot[2 * d + 1] * SLOT - count
        for b in range(16):
            dp[k, b] = bq[jnp.where(b < count, near, far) + b]

    def send_d(k):
        fill_d(k)
        d4(k).start()

    run(1, send_d)
    fill_d(0)
    own_d.start()

    def drain(k):
        q1(k).wait_send()
        c1(k).wait_send()
        q2(k).wait_send()
        c2(k).wait_send()
        d3(k).wait_send()
        out_k(k).wait()
        out_v(k).wait()
        d4(k).wait_send()
        d4(k).wait_recv()

    run(1, drain)
    out_k(0).wait()
    out_v(0).wait()
    own_d.wait()


def local(
    enc_keys, enc_values, dec_queries, cotangent,
    input_lengths, target_lengths, enc_pack, dec_pack, task_group, dro_weights,
):
    me = lax.axis_index("pack")
    lens_e, lens_d = input_lengths[0], target_lengths[0]
    ep, dpk, task = enc_pack[0], dec_pack[0], task_group[0, :, 0]
    ordinal = jnp.arange(64, dtype=jnp.int32)
    earlier = ordinal[None, :] < ordinal[:, None]
    same_e = earlier & (ep[:, None] == ep[None, :])
    same_d = earlier & (dpk[:, None] == dpk[None, :])
    slot_e = ep * 2 + jnp.sum(same_e, axis=1).astype(jnp.int32)
    slot_d = dpk * 2 + jnp.sum(same_d, axis=1).astype(jnp.int32)
    start_d = dpk * 16 + jnp.sum(jnp.where(same_d, lens_d[None, :], 0), axis=1) // 8
    at_e = slot_e[None, :] == ordinal[:, None]
    at_d = slot_d[None, :] == ordinal[:, None]

    def pick(at, values):
        return jnp.sum(jnp.where(at, values[None, :], 0), axis=1)

    qstart = pick(at_e, start_d)
    qlen = pick(at_e, lens_d)
    klen = pick(at_e, lens_e)
    qgroup = pick(at_e, task)
    eslot = pick(at_d, slot_e)
    dlen = pick(at_d, lens_d)
    first = dlen.reshape(NP, 2)[:, 0] // 8

    group_index = jnp.arange(GROUPS, dtype=jnp.int32)
    part = jnp.sum(jnp.where(task[:, None] == group_index[None, :], lens_d[:, None], 0), axis=0)
    counts = lax.psum(part.astype(jnp.float32), "dp")
    weights = dro_weights.astype(jnp.float32)
    total = 128 * NP * lax.axis_size("dp")
    scales = weights / jnp.sum(weights) * (total / counts)

    own_len = lax.dynamic_slice_in_dim(qlen, 2 * me, 2)
    own_keys = lax.dynamic_slice_in_dim(klen, 2 * me, 2)
    own_group = lax.dynamic_slice_in_dim(qgroup, 2 * me, 2)
    mine = jnp.concatenate([own_len, own_keys])
    own_match = own_group[:, None] == group_index[None, :]
    own_scale = jnp.sum(jnp.where(own_match, scales[None, :], 0.0), axis=1)

    bf = jnp.bfloat16
    smem = pl.BlockSpec(memory_space=pltpu.SMEM)
    hbm = pl.BlockSpec(memory_space=pl.ANY)
    dma = pltpu.SemaphoreType.DMA
    dq, dk, dv, loss = pl.pallas_call(
        kernel,
        out_shape=(
            jax.ShapeDtypeStruct((16, 8, 4096), bf),
            jax.ShapeDtypeStruct((256, 4096), bf),
            jax.ShapeDtypeStruct((256, 4096), bf),
            jax.ShapeDtypeStruct((1, 256), jnp.float32),
        ),
        in_specs=[smem] * 5 + [hbm] * 4,
        out_specs=(hbm, hbm, hbm, pl.BlockSpec(memory_space=pltpu.VMEM)),
        scratch_shapes=[
            pltpu.VMEM((256, 4096), bf),
            pltpu.VMEM((256, 4096), bf),
            pltpu.VMEM((TABLE + 16, 8, 128), bf),
            pltpu.VMEM((TABLE + 16, 8, 128), bf),
            pltpu.VMEM((NP, PAIR, 8, 128), bf),
            pltpu.VMEM((NP, PAIR, 8, 128), bf),
            pltpu.VMEM((NP, PAIR, 8, 128), bf),
            pltpu.VMEM((NP, PAIR, 8, 128), bf),
            pltpu.VMEM((NP, PAIR, 8, 128), bf),
            pltpu.VMEM((NP * PAIR, 8, 128), bf),
            pltpu.VMEM((NP, 16, 8, 128), bf),
            pltpu.VMEM((NP, 256, 128), bf),
            pltpu.VMEM((NP, 256, 128), bf),
            dma((8,)),
        ] + [dma((NP,))] * 14,
        compiler_params=pltpu.CompilerParams(
            collective_id=0, has_side_effects=True, vmem_limit_bytes=56 * 1024 * 1024
        ),
        cost_estimate=pl.CostEstimate(flops=3_000_000_000, bytes_accessed=11_000_000, transcendentals=4_000_000),
    )(
        qstart, eslot, first, mine, own_scale,
        enc_keys, enc_values,
        dec_queries.reshape(16, 8, 4096), cotangent.reshape(16, 8, 4096),
    )
    token_loss = loss[0]
    example_loss = jnp.stack([jnp.sum(token_loss[:120]), jnp.sum(token_loss[120:])])
    loss_part = jnp.sum(jnp.where(own_match, example_loss[:, None], 0.0), axis=0)
    group_loss = lax.psum(loss_part, ("dp", "pack")) / counts
    return dq.reshape(128, 4096), dk, dv, group_loss


def solution(mesh):
    rows = P(("dp", "pack"), None)
    small = P("dp", None)
    return jax.shard_map(
        local,
        mesh=mesh,
        in_specs=(rows, rows, rows, rows, small, small, small, small, P("dp", None, None), P()),
        out_specs=(rows, rows, rows, P()),
        check_vma=False,
    )
```

time: 2040 us -> 263 us (0.13); the launches traced: 2000 us -> 263 us
  loops' own time: 733 us -> 0 us
  local copies, waits for them, and re-layouts: 689 us -> 6.38 us
  matrix products: 201 us -> 0 us
  Pallas kernels: 0 us -> 147 us
  other arithmetic: 140 us -> 15.8 us
  waiting for transfers between devices: 82.5 us -> 0 us
  starting transfers between devices: 48.1 us -> 0 us
    another operation x3 -> x0, loops' own time: 733 us -> none  [the longest x1 250 us: local(): lax.scan(output_step, attended_start, (attention_store, key_start_blocks,...]
    dynamic_update_slice x288 -> x0, local copies, waits for them, and re-layouts: 301 us -> none  [the longest x256 281 us: put_rows(): buffer = lax.dynamic_update_slice_in_dim(buffer, merged, starts[item], 0)]
    dynamic_slice x386 -> x3, local copies, waits for them, and re-layouts: 208 us -> 0.22 us  [the longest x1 0.07 us: local(): own_group = lax.dynamic_slice_in_dim(qgroup, 2 * me, 2)]
    pallas_call x0 -> x1, Pallas kernels: none -> 147 us  [local(): pl.pallas_call(kernel, out_shape=(jax.ShapeDtypeStruct((16, 8, 4096), bf)...]
    select_n x193 -> x1, other arithmetic: 131 us -> 0.53 us  [local(): first = dlen.reshape(NP, 2)[:, 0] // 8]
    dot_general x160 -> x0, matrix products: 127 us -> none  [the longest x32 42.3 us: backward_step(): jnp.einsum('eqhd,ekhd->ehqk', gradient_split, value_split, preferred_elem...]
    slice x359 -> x1, local copies, waits for them, and re-layouts: 116 us -> 0.11 us  [local(): first = dlen.reshape(NP, 2)[:, 0] // 8]
    all_to_all x8 -> x0, waiting for transfers between devices: 82.5 us -> none  [the longest x1 22.7 us: local(): lax.all_to_all(key_result, 'pack', split_axis=0, concat_axis=1, tiled=True)]
  transfers between devices with their start and end apart: 8 -> 0, of which waited for: 5 -> 0; matrix products, arithmetic and copies ran while one was open for 9% -> 0% of each run, Pallas kernels for 0% -> 0%
where the time goes in v1:
time: 263 us
  Pallas kernels  147 us (56%)
  blocking collectives  93 us (35%)
  other arithmetic  15.8 us (6%)
  local copies, waits for them, and re-layouts  6.38 us (2%)
    pallas_call x1, Pallas kernels, local(): pl.pallas_call(kernel, out_shape=(jax.ShapeDtypeStruct((16, 8, 4096), bf)...  147 us
    psum x1, blocking collectives, local(): group_loss = lax.psum(loss_part, ('dp', 'pack')) / counts  75.7 us
    psum x1, blocking collectives, local(): counts = lax.psum(part.astype(jnp.float32), 'dp')  17.3 us
    unnamed x7, local copies, waits for them, and re-layouts  5.96 us

profile of v1, /device:TPU:1, one launch (start us, length us, event | category | flops | bytes accessed | tf_op | source)
XLA Modules:
  0.0 263.0 jit_solution(1018101534188134724)
XLA Ops:
  0.6 1.3 convert_reduce_fusion.2
  1.9 0.8 select_reduce_fusion.7
  2.7 17.3 %psum.14 = f32[16]{0:T(128)S(1)} all-reduce(f32[16]{0:T(128)S(1)} %convert_element_type.15), channel_id=1, replica_groups=mesh['dp'=8,'pack'=32] {'dp'}, use_global_device_ids=true, to_apply=%region_11.12 | all-reduce | flops 16 | bytes 128 | tf_op jit(solution)/shard_map/psum | solution.py:309
  20.0 1.3 divide_multiply_fusion
  21.3 0.9 convert_reduce_fusion.1
  22.2 0.7 fusion.3
  22.9 0.9 convert_reduce_fusion
  23.8 0.7 fusion.2
  24.5 1.4 select_reduce_fusion
  26.0 0.8 select_reduce_fusion.9.scale
  26.9 0.6 pad_add_fusion.mine
  27.5 0.7 add_bitcast_fusion
  28.1 0.6 select_reduce_fusion.5.qstart
  29.0 0.5 and_select_fusion.first
  29.5 147.1 %shard_map.129 = (bf16[16,8,4096]{2,1,0:T(8,128)(2,1)}, bf16[256,4096]{1,0:T(8,128)(2,1)}, bf16[256,4096]{1,0:T(8,128)(2,1)}, f32[1,256]{1,0:T(1,128)}) custom-call(s32[64]{0:T(128)} %select_reduce_fusion.5.qstart, s32[64]{0:T(128)} %get-tuple-element.13.eslot, s32[32]{0:T(128)} %and_select_fusion.first, s32[4]{0:T(128)} %pad_add_fusion.mine, ...), custom_call_target="tpu_custom_call" | custom-call | flops 3000000000 | bytes 11000000 | tf_op jit(solution)/shard_map/pallas_call | solution.py:325
  176.7 1.5 slice_reduce_fusion.1
  178.1 1.2 slice_reduce_fusion.2
  179.4 1.4 pad_maximum_fusion
  180.8 75.7 %psum.15 = f32[16]{0:T(128)S(1)} all-reduce(f32[16]{0:T(128)S(1)} %select_reduce_fusion.8), channel_id=1, replica_groups=mesh['dp'=8,'pack'=32] {'dp','pack'}, use_global_device_ids=true, to_apply=%region_16.17 | all-reduce | flops 16 | bytes 128 | tf_op jit(solution)/shard_map/psum | solution.py:363
  256.5 0.5 div.47
  257.0 2.3 copy.17
  259.3 1.3 copy.18
  260.6 1.0 copy-done
  261.7 1.3 copy.19
  (10 shorter events, 0.5 us)
Async XLA Ops:
  176.6 82.7 %copy-start.1 = (bf16[256,4096]{1,0:T(8,128)(2,1)S(1)}, bf16[256,4096]{1,0:T(8,128)(2,1)}, u32[]{:S(2)}) copy-start(bf16[256,4096]{1,0:T(8,128)(2,1)} %get-tuple-element.23) | copy-start | bytes 6291460
  259.3 2.3 copy-start

commit v2 on v1

--- a/solution.py
+++ b/solution.py
@@ -17,22 +17,36 @@
 
 
 def kernel(
-    qstart, eslot, first, mine, scale,
+    lens_e_ref, lens_d_ref, ep_ref, dpk_ref, task_ref, dro_ref,
     k_hbm, v_hbm, q_hbm, c_hbm,
     dq_out, dk_out, dv_out, loss_out,
     kv, vv, qt, ct, sq, sc, qin, cin, sd, bq, dp, dks, dvs,
-    lsem, s1q, r1q, s1c, r1c, s2q, r2q, s2c, r2c, s3, r3, s4, r4, ksem, vsem,
+    tab_v, tab, cnt, lpart, lz,
+    lsem, s1q, r1q, s1c, r1c, s2q, r2q, s2c, r2c, s3, r3, s4, r4, ksem, vsem, sl, rl, szc, rzc, szl, rzl,
 ):
     me = lax.axis_index("pack")
+    z = lax.axis_index("dp")
+    nz = lax.axis_size("dp")
+    x, y, core = me // 8, lax.rem(me // 2, 4), lax.rem(me, 2)
+
+    def other(k, source):
+        j = k // 2
+        dx, dy = lax.rem(j, 4), lax.rem(j // 4 + j, 4)
+        far = lax.rem(core + k, 2)
+        sign = (2 * far - 1) if source else (1 - 2 * core)
+        return lax.rem(x + sign * dx + 4, 4) * 8 + lax.rem(y + sign * dy + 4, 4) * 2 + far
 
     def peer(k):
-        return lax.rem(me + k, NP)
+        return other(k, False)
 
     def back(k):
-        return lax.rem(me - k + NP, NP)
+        return other(k, True)
 
     def cols(i):
         return pl.ds(pl.multiple_of(i * 128, 128), 128)
+
+    def zpeer(k):
+        return lax.rem(z + k, nz)
 
     load_k = pltpu.make_async_copy(k_hbm, kv, lsem.at[0])
     load_v = pltpu.make_async_copy(v_hbm, vv, lsem.at[1])
@@ -43,8 +57,13 @@
         pl.semaphore_signal(barrier, inc=1, device_id={"pack": peer(k)}, device_id_type=MESH)
         return carry
 
+    def greet_z(k, carry):
+        pl.semaphore_signal(barrier, inc=1, device_id={"dp": zpeer(k)}, device_id_type=MESH)
+        return carry
+
     lax.fori_loop(1, NP, greet, 0)
-    pl.semaphore_wait(barrier, NP - 1)
+    lax.fori_loop(1, nz, greet_z, 0)
+    pl.semaphore_wait(barrier, NP + nz - 2)
 
     def spread(src, dst, send, recv):
         def make(k):
@@ -76,6 +95,75 @@
     load_v.start()
     qt[pl.ds(TABLE, 16)] = jnp.zeros((16, 8, 128), jnp.bfloat16)
     ct[pl.ds(TABLE, 16)] = jnp.zeros((16, 8, 128), jnp.bfloat16)
+    bq[pl.ds(NP * PAIR, 16)] = jnp.zeros((16, 8, 128), jnp.bfloat16)
+
+    f32 = jnp.float32
+    i32 = jnp.int32
+    lens_e_r = lens_e_ref[...]
+    lens_d_r = lens_d_ref[...]
+    ep_r = ep_ref[...]
+    dpk_r = dpk_ref[...]
+    at_row = lax.broadcasted_iota(i32, (64, 64), 0)
+    at_col = lax.broadcasted_iota(i32, (64, 64), 1)
+
+    def column(row):
+        return jnp.sum(jnp.where(at_row == at_col, row, 0), axis=1, keepdims=True)
+
+    lens_d_c = column(lens_d_r)
+    group = lax.broadcasted_iota(i32, (64, 128), 1)
+    part = jnp.sum(jnp.where(column(task_ref[...]) == group, lens_d_c, 0), axis=0, keepdims=True)
+    cnt[z] = jnp.broadcast_to(part.astype(f32), (8, 128))
+
+    def count_copy(k):
+        return pltpu.make_async_remote_copy(
+            src_ref=cnt.at[z],
+            dst_ref=cnt.at[z],
+            send_sem=szc.at[k],
+            recv_sem=rzc.at[k],
+            device_id={"dp": zpeer(k)},
+            device_id_type=MESH,
+        )
+
+    def count_arrival(k):
+        source = lax.rem(z - k + nz, nz)
+        return pltpu.make_async_remote_copy(
+            src_ref=cnt.at[source],
+            dst_ref=cnt.at[source],
+            send_sem=szc.at[k],
+            recv_sem=rzc.at[k],
+            device_id={"dp": source},
+            device_id_type=MESH,
+        )
+
+    def run_z(body):
+        def step(k, carry):
+            body(k)
+            return carry
+        lax.fori_loop(1, nz, step, 0)
+
+    run_z(lambda k: count_copy(k).start())
+
+    ahead_e = jnp.where(column(ep_r) == ep_r, jnp.where(at_row < at_col, 1, 0), 0)
+    ahead_d = jnp.where(column(dpk_r) == dpk_r, jnp.where(at_row < at_col, 1, 0), 0)
+    slot_e_r = 2 * ep_r + jnp.sum(ahead_e, axis=0, keepdims=True)
+    slot_d_r = 2 * dpk_r + jnp.sum(ahead_d, axis=0, keepdims=True)
+    start_r = 16 * dpk_r + jnp.sum(ahead_d * lens_d_c, axis=0, keepdims=True) // 8
+
+    def pick(slot_r, values_r):
+        return jnp.sum(jnp.where(slot_r == at_row, values_r, 0), axis=1, keepdims=True)
+
+    columns = (
+        pick(slot_e_r, start_r), pick(slot_e_r, lens_d_r), pick(slot_e_r, lens_e_r), pick(slot_e_r, task_ref[...]),
+        pick(slot_d_r, slot_e_r), pick(slot_d_r, lens_d_r),
+    )
+    wide = jnp.zeros((64, 128), i32)
+    for at, values in enumerate(columns):
+        wide = jnp.where(group == at, values, wide)
+    wide = jnp.concatenate([wide, jnp.zeros((64, 128), i32)], axis=0)
+    tab_v[...] = wide.T[:8]
+    table_copy = pltpu.make_async_copy(tab_v, tab, lsem.at[5])
+    table_copy.start()
+    table_copy.wait()
 
     def deal(table, send_buf, into, send, recv):
         def make(k):
@@ -91,7 +179,7 @@
         def fill(k, dst):
             p = peer(k)
             for a in range(2):
-                start = qstart[2 * p + a]
+                start = jnp.clip(tab[0, 2 * p + a], 0, TABLE)
                 dst[k, pl.ds(a * SLOT, SLOT)] = table[pl.ds(start, SLOT)]
 
         return make, fill
@@ -124,11 +212,20 @@
     load_k.wait()
     load_v.wait()
 
-    len0 = mine[0]
-    len1 = mine[1]
-    keys0 = mine[2]
-    scale0 = scale[0]
-    scale1 = scale[1]
+    len0 = tab[1, 2 * me]
+    len1 = tab[1, 2 * me + 1]
+    keys0 = tab[2, 2 * me]
+    run_z(lambda k: count_arrival(k).wait_recv())
+    counts = cnt[0][:1]
+    for at in range(1, nz):
+        counts = counts + cnt[at][:1]
+    lane_r = lax.broadcasted_iota(jnp.int32, (1, 128), 1)
+    weights = jnp.concatenate([dro_ref[...].astype(f32), jnp.zeros((1, 128 - GROUPS), f32)], axis=1)
+    scales = weights / jnp.sum(weights, axis=1, keepdims=True) * (128.0 * NP * nz / counts)
+    own0 = lane_r == tab[3, 2 * me]
+    own1 = lane_r == tab[3, 2 * me + 1]
+    scale0 = jnp.sum(jnp.where(own0, scales, 0.0), axis=1, keepdims=True)
+    scale1 = jnp.sum(jnp.where(own1, scales, 0.0), axis=1, keepdims=True)
     place_c = lax.broadcasted_iota(jnp.int32, (256, 1), 0)
     place_r = lax.broadcasted_iota(jnp.int32, (1, 256), 1)
 
@@ -227,7 +324,33 @@
         return loss
 
     loss = lax.fori_loop(1, NP, pair_step, loss)
-    loss_out[...] = jnp.where(live_r > 0.5, loss, 0.0)
+    loss = jnp.where(live_r > 0.5, loss, 0.0)
+    loss0 = jnp.sum(jnp.where(place_r < 120, loss, 0.0), axis=1, keepdims=True)
+    loss1 = jnp.sum(jnp.where(place_r < 120, 0.0, loss), axis=1, keepdims=True)
+    own_loss = jnp.where(own0, loss0, 0.0) + jnp.where(own1, loss1, 0.0)
+    lpart[me] = jnp.broadcast_to(own_loss, (8, 128))
+
+    def loss_copy(k):
+        return pltpu.make_async_remote_copy(
+            src_ref=lpart.at[me],
+            dst_ref=lpart.at[me],
+            send_sem=sl.at[k],
+            recv_sem=rl.at[k],
+            device_id={"pack": peer(k)},
+            device_id_type=MESH,
+        )
+
+    def loss_arrival(k):
+        return pltpu.make_async_remote_copy(
+            src_ref=lpart.at[back(k)],
+            dst_ref=lpart.at[back(k)],
+            send_sem=sl.at[k],
+            recv_sem=rl.at[k],
+            device_id={"pack": back(k)},
+            device_id_type=MESH,
+        )
+
+    run(1, lambda k: loss_copy(k).start())
 
     run(1, lambda k: d3(k).wait_recv())
 
@@ -245,11 +368,11 @@
 
     def fill_d(k):
         d = peer(k)
-        near = eslot[2 * d] * SLOT
-        count = first[d]
-        far = eslot[2 * d + 1] * SLOT - count
+        near = tab[4, 2 * d] * SLOT
+        count = tab[5, 2 * d] // 8
+        far = tab[4, 2 * d + 1] * SLOT - count
         for b in range(16):
-            dp[k, b] = bq[jnp.where(b < count, near, far) + b]
+            dp[k, b] = bq[jnp.clip(jnp.where(b < count, near, far) + b, 0, NP * PAIR - 1)]
 
     def send_d(k):
         fill_d(k)
@@ -259,7 +382,43 @@
     fill_d(0)
     own_d.start()
 
+    run(1, lambda k: loss_arrival(k).wait_recv())
+    lz[z] = jnp.sum(lpart[...], axis=0)
+
+    def zloss_copy(k):
+        return pltpu.make_async_remote_copy(
+            src_ref=lz.at[z],
+            dst_ref=lz.at[z],
+            send_sem=szl.at[k],
+            recv_sem=rzl.at[k],
+            device_id={"dp": zpeer(k)},
+            device_id_type=MESH,
+        )
+
+    def zloss_arrival(k):
+        source = lax.rem(z - k + nz, nz)
+        return pltpu.make_async_remote_copy(
+            src_ref=lz.at[source],
+            dst_ref=lz.at[source],
+            send_sem=szl.at[k],
+            recv_sem=rzl.at[k],
+            device_id={"dp": source},
+            device_id_type=MESH,
+        )
+
+    run_z(lambda k: zloss_copy(k).start())
+    run_z(lambda k: zloss_arrival(k).wait_recv())
+    total = jnp.sum(lz[...], axis=0)[:1] / counts
+    loss_out[...] = total[:, :GROUPS]
+
+    def drain_z(k):
+        count_copy(k).wait_send()
+        zloss_copy(k).wait_send()
+
+    run_z(drain_z)
+
     def drain(k):
+        loss_copy(k).wait_send()
         q1(k).wait_send()
         c1(k).wait_send()
         q2(k).wait_send()
@@ -280,47 +439,10 @@
     enc_keys, enc_values, dec_queries, cotangent,
     input_lengths, target_lengths, enc_pack, dec_pack, task_group, dro_weights,
 ):
-    me = lax.axis_index("pack")
-    lens_e, lens_d = input_lengths[0], target_lengths[0]
-    ep, dpk, task = enc_pack[0], dec_pack[0], task_group[0, :, 0]
-    ordinal = jnp.arange(64, dtype=jnp.int32)
-    earlier = ordinal[None, :] < ordinal[:, None]
-    same_e = earlier & (ep[:, None] == ep[None, :])
-    same_d = earlier & (dpk[:, None] == dpk[None, :])
-    slot_e = ep * 2 + jnp.sum(same_e, axis=1).astype(jnp.int32)
-    slot_d = dpk * 2 + jnp.sum(same_d, axis=1).astype(jnp.int32)
-    start_d = dpk * 16 + jnp.sum(jnp.where(same_d, lens_d[None, :], 0), axis=1) // 8
-    at_e = slot_e[None, :] == ordinal[:, None]
-    at_d = slot_d[None, :] == ordinal[:, None]
-
-    def pick(at, values):
-        return jnp.sum(jnp.where(at, values[None, :], 0), axis=1)
-
-    qstart = pick(at_e, start_d)
-    qlen = pick(at_e, lens_d)
-    klen = pick(at_e, lens_e)
-    qgroup = pick(at_e, task)
-    eslot = pick(at_d, slot_e)
-    dlen = pick(at_d, lens_d)
-    first = dlen.reshape(NP, 2)[:, 0] // 8
-
-    group_index = jnp.arange(GROUPS, dtype=jnp.int32)
-    part = jnp.sum(jnp.where(task[:, None] == group_index[None, :], lens_d[:, None], 0), axis=0)
-    counts = lax.psum(part.astype(jnp.float32), "dp")
-    weights = dro_weights.astype(jnp.float32)
-    total = 128 * NP * lax.axis_size("dp")
-    scales = weights / jnp.sum(weights) * (total / counts)
-
-    own_len = lax.dynamic_slice_in_dim(qlen, 2 * me, 2)
-    own_keys = lax.dynamic_slice_in_dim(klen, 2 * me, 2)
-    own_group = lax.dynamic_slice_in_dim(qgroup, 2 * me, 2)
-    mine = jnp.concatenate([own_len, own_keys])
-    own_match = own_group[:, None] == group_index[None, :]
-    own_scale = jnp.sum(jnp.where(own_match, scales[None, :], 0.0), axis=1)
-
     bf = jnp.bfloat16
-    smem = pl.BlockSpec(memory_space=pltpu.SMEM)
+    vmem = pl.BlockSpec(memory_space=pltpu.VMEM)
     hbm = pl.BlockSpec(memory_space=pl.ANY)
+    nz = lax.axis_size("dp")
     dma = pltpu.SemaphoreType.DMA
     dq, dk, dv, loss = pl.pallas_call(
         kernel,
@@ -328,10 +450,10 @@
             jax.ShapeDtypeStruct((16, 8, 4096), bf),
             jax.ShapeDtypeStruct((256, 4096), bf),
             jax.ShapeDtypeStruct((256, 4096), bf),
-            jax.ShapeDtypeStruct((1, 256), jnp.float32),
+            jax.ShapeDtypeStruct((1, GROUPS), jnp.float32),
         ),
-        in_specs=[smem] * 5 + [hbm] * 4,
-        out_specs=(hbm, hbm, hbm, pl.BlockSpec(memory_space=pltpu.VMEM)),
+        in_specs=[vmem] * 6 + [hbm] * 4,
+        out_specs=(hbm, hbm, hbm, vmem),
         scratch_shapes=[
             pltpu.VMEM((256, 4096), bf),
             pltpu.VMEM((256, 4096), bf),
@@ -342,26 +464,27 @@
             pltpu.VMEM((NP, PAIR, 8, 128), bf),
             pltpu.VMEM((NP, PAIR, 8, 128), bf),
             pltpu.VMEM((NP, PAIR, 8, 128), bf),
-            pltpu.VMEM((NP * PAIR, 8, 128), bf),
+            pltpu.VMEM((NP * PAIR + 16, 8, 128), bf),
             pltpu.VMEM((NP, 16, 8, 128), bf),
             pltpu.VMEM((NP, 256, 128), bf),
             pltpu.VMEM((NP, 256, 128), bf),
+            pltpu.VMEM((8, 128), jnp.int32),
+            pltpu.SMEM((8, 128), jnp.int32),
+            pltpu.VMEM((nz, 8, 128), jnp.float32),
+            pltpu.VMEM((NP, 8, 128), jnp.float32),
+            pltpu.VMEM((nz, 8, 128), jnp.float32),
             dma((8,)),
-        ] + [dma((NP,))] * 14,
+        ] + [dma((NP,))] * 16 + [dma((nz,))] * 4,
         compiler_params=pltpu.CompilerParams(
             collective_id=0, has_side_effects=True, vmem_limit_bytes=56 * 1024 * 1024
         ),
         cost_estimate=pl.CostEstimate(flops=3_000_000_000, bytes_accessed=11_000_000, transcendentals=4_000_000),
     )(
-        qstart, eslot, first, mine, own_scale,
+        input_lengths, target_lengths, enc_pack, dec_pack, task_group.reshape(1, 64), dro_weights.reshape(1, GROUPS),
         enc_keys, enc_values,
         dec_queries.reshape(16, 8, 4096), cotangent.reshape(16, 8, 4096),
     )
-    token_loss = loss[0]
-    example_loss = jnp.stack([jnp.sum(token_loss[:120]), jnp.sum(token_loss[120:])])
-    loss_part = jnp.sum(jnp.where(own_match, example_loss[:, None], 0.0), axis=0)
-    group_loss = lax.psum(loss_part, ("dp", "pack")) / counts
-    return dq.reshape(128, 4096), dk, dv, group_loss
+    return dq.reshape(128, 4096), dk, dv, loss.reshape(GROUPS)
 
 
 def solution(mesh):

time: 263 us -> 138 us (0.52)
  blocking collectives: 93 us -> 0 us
  Pallas kernels: 147 us -> 130 us
  other arithmetic: 15.8 us -> 0 us
    psum x2 -> x0, blocking collectives: 93 us -> none  [the longest x1 75.7 us: local(): group_loss = lax.psum(loss_part, ('dp', 'pack')) / counts]
    pallas_call x1, Pallas kernels: 147 us -> 130 us  [local(): pl.pallas_call(kernel, out_shape=(jax.ShapeDtypeStruct((16, 8, 4096), bf)...]
    reduce_sum x10 -> x0, other arithmetic: 9.5 us -> none  [the longest x2 2.06 us: pick(): return jnp.sum(jnp.where(at, values[None, :], 0), axis=1)]
    unnamed x7 -> x10, local copies, waits for them, and re-layouts: 5.96 us -> 6.62 us
where the time goes in v2:
time: 138 us
  Pallas kernels  130 us (94%)
  local copies, waits for them, and re-layouts  6.62 us (5%)
    pallas_call x1, Pallas kernels, local(): pl.pallas_call(kernel, out_shape=(jax.ShapeDtypeStruct((16, 8, 4096), bf)...  130 us
    unnamed x10, local copies, waits for them, and re-layouts  6.62 us

profile of v2, /device:TPU:1, one launch (start us, length us, event | category | flops | bytes accessed | tf_op | source)
XLA Modules:
  0.0 137.6 jit_solution(5877355421992123970)
XLA Ops:
  0.6 130.4 %shard_map.129 = (bf16[16,8,4096]{2,1,0:T(8,128)(2,1)}, bf16[256,4096]{1,0:T(8,128)(2,1)}, bf16[256,4096]{1,0:T(8,128)(2,1)}, f32[1,16]{1,0:T(1,128)}) custom-call(s32[1,64]{1,0:T(1,128)} %lens_e_ref.1, s32[1,64]{1,0:T(1,128)} %lens_d_ref.1, s32[1,64]{1,0:T(1,128)} %ep_ref.1, s32[1,64]{1,0:T(1,128)} %dpk_ref.1, s32[1,64]{1,0:T(1,128)} %bitcast.9, ...), custom_call_target="tpu_custom_call" | custom-call | flops 3000000000 | bytes 11000000 | tf_op jit(solution)/shard_map/pallas_call | solution.py:447
  131.0 0.0 copy-start.1
  131.0 2.4 %copy.18 = bf16[128,4096]{1,0:T(8,128)(2,1)} copy(bf16[128,4096]{1,0:T(8,128)(2,1)} %bitcast.6) | data formatting | bytes 2097152
  133.4 0.0 copy-done.1
  133.4 0.0 copy-start
  133.4 1.3 copy.19
  134.8 1.0 copy-done
  135.8 0.0 copy-start.2
  135.8 1.3 copy.20
  137.1 0.0 copy-done.2
  137.1 0.5 copy.21
Async XLA Ops:
  131.0 2.4 %copy-start.1 = (bf16[256,4096]{1,0:T(8,128)(2,1)S(1)}, bf16[256,4096]{1,0:T(8,128)(2,1)}, u32[]{:S(2)}) copy-start(bf16[256,4096]{1,0:T(8,128)(2,1)} %get-tuple-element.17) | copy-start | bytes 6291460
  133.4 2.3 %copy-start = (bf16[256,4096]{1,0:T(8,128)(2,1)S(1)}, bf16[256,4096]{1,0:T(8,128)(2,1)}, u32[]{:S(2)}) copy-start(bf16[256,4096]{1,0:T(8,128)(2,1)} %get-tuple-element.18) | copy-start | bytes 6291460
  135.8 1.3 copy-start.2

commit v3 on v2

--- a/solution.py
+++ b/solution.py
@@ -20,10 +20,13 @@
     lens_e_ref, lens_d_ref, ep_ref, dpk_ref, task_ref, dro_ref,
     k_hbm, v_hbm, q_hbm, c_hbm,
     dq_out, dk_out, dv_out, loss_out,
-    kv, vv, qt, ct, sq, sc, qin, cin, sd, bq, dp, dks, dvs,
-    tab_v, tab, cnt, lpart, lz,
-    lsem, s1q, r1q, s1c, r1c, s2q, r2q, s2c, r2c, s3, r3, s4, r4, ksem, vsem, sl, rl, szc, rzc, szl, rzl,
+    kv, vv, qt, ct, sq, sc, qin, cin, sd, bq, dp,
+    tab_v, tab, cnt, lpart, lz, ctot, ltot,
+    lsem, one, r2q, r2c,
 ):
+    s1q, r1q, s1c, r1c, s2q, s2c, s3, r3, s4, r4, sl, rl, szc, rzc, szl, rzl, szt, rzt, szm, rzm = (
+        one.at[at] for at in range(20)
+    )
     me = lax.axis_index("pack")
     z = lax.axis_index("dp")
     nz = lax.axis_size("dp")
@@ -45,6 +48,8 @@
     def cols(i):
         return pl.ds(pl.multiple_of(i * 128, 128), 128)
 
+    hub = nz - 1
+
     def zpeer(k):
         return lax.rem(z + k, nz)
 
@@ -57,46 +62,9 @@
         pl.semaphore_signal(barrier, inc=1, device_id={"pack": peer(k)}, device_id_type=MESH)
         return carry
 
-    def greet_z(k, carry):
-        pl.semaphore_signal(barrier, inc=1, device_id={"dp": zpeer(k)}, device_id_type=MESH)
-        return carry
-
     lax.fori_loop(1, NP, greet, 0)
-    lax.fori_loop(1, nz, greet_z, 0)
-    pl.semaphore_wait(barrier, NP + nz - 2)
-
-    def spread(src, dst, send, recv):
-        def make(k):
-            return pltpu.make_async_remote_copy(
-                src_ref=src.at[:, :, cols(peer(k))],
-                dst_ref=dst.at[pl.ds(me * 16, 16)],
-                send_sem=send.at[k],
-                recv_sem=recv.at[k],
-                device_id={"pack": peer(k)},
-                device_id_type=MESH,
-            )
-        return make
-
-    def run(count_from, body):
-        def step(k, carry):
-            body(k)
-            return carry
-        lax.fori_loop(count_from, NP, step, 0)
-
-    q1 = spread(q_hbm, qt, s1q, r1q)
-    c1 = spread(c_hbm, ct, s1c, r1c)
-    own_q = pltpu.make_async_copy(q_hbm.at[:, :, cols(me)], qt.at[pl.ds(me * 16, 16)], lsem.at[2])
-    own_c = pltpu.make_async_copy(c_hbm.at[:, :, cols(me)], ct.at[pl.ds(me * 16, 16)], lsem.at[3])
-    run(1, lambda k: q1(k).start())
-    own_q.start()
-    run(1, lambda k: c1(k).start())
-    own_c.start()
     load_k.start()
     load_v.start()
-    qt[pl.ds(TABLE, 16)] = jnp.zeros((16, 8, 128), jnp.bfloat16)
-    ct[pl.ds(TABLE, 16)] = jnp.zeros((16, 8, 128), jnp.bfloat16)
-    bq[pl.ds(NP * PAIR, 16)] = jnp.zeros((16, 8, 128), jnp.bfloat16)
-
     f32 = jnp.float32
     i32 = jnp.int32
     lens_e_r = lens_e_ref[...]
@@ -113,35 +81,6 @@
     group = lax.broadcasted_iota(i32, (64, 128), 1)
     part = jnp.sum(jnp.where(column(task_ref[...]) == group, lens_d_c, 0), axis=0, keepdims=True)
     cnt[z] = jnp.broadcast_to(part.astype(f32), (8, 128))
-
-    def count_copy(k):
-        return pltpu.make_async_remote_copy(
-            src_ref=cnt.at[z],
-            dst_ref=cnt.at[z],
-            send_sem=szc.at[k],
-            recv_sem=rzc.at[k],
-            device_id={"dp": zpeer(k)},
-            device_id_type=MESH,
-        )
-
-    def count_arrival(k):
-        source = lax.rem(z - k + nz, nz)
-        return pltpu.make_async_remote_copy(
-            src_ref=cnt.at[source],
-            dst_ref=cnt.at[source],
-            send_sem=szc.at[k],
-            recv_sem=rzc.at[k],
-            device_id={"dp": source},
-            device_id_type=MESH,
-        )
-
-    def run_z(body):
-        def step(k, carry):
-            body(k)
-            return carry
-        lax.fori_loop(1, nz, step, 0)
-
-    run_z(lambda k: count_copy(k).start())
 
     ahead_e = jnp.where(column(ep_r) == ep_r, jnp.where(at_row < at_col, 1, 0), 0)
     ahead_d = jnp.where(column(dpk_r) == dpk_r, jnp.where(at_row < at_col, 1, 0), 0)
@@ -163,14 +102,82 @@
     tab_v[...] = wide.T[:8]
     table_copy = pltpu.make_async_copy(tab_v, tab, lsem.at[5])
     table_copy.start()
-    table_copy.wait()
+    pl.semaphore_wait(barrier, jnp.where(z == hub, NP + nz - 2, NP - 1))
+
+    @pl.when(z != hub)
+    def _():
+        pl.semaphore_signal(barrier, inc=1, device_id={"dp": hub}, device_id_type=MESH)
+
+
+    def spread(src, dst, send, recv):
+        def make(k):
+            return pltpu.make_async_remote_copy(
+                src_ref=src.at[:, :, cols(peer(k))],
+                dst_ref=dst.at[pl.ds(me * 16, 16)],
+                send_sem=send,
+                recv_sem=recv,
+                device_id={"pack": peer(k)},
+                device_id_type=MESH,
+            )
+        return make
+
+    def run(count_from, body, unroll=False):
+        def step(k, carry):
+            body(k)
+            return carry
+        lax.fori_loop(count_from, NP, step, 0, unroll=unroll)
+
+    def total(buffer, send, recv):
+        return pltpu.make_async_remote_copy(
+            src_ref=buffer, dst_ref=buffer, send_sem=send, recv_sem=recv,
+            device_id={"pack": peer(1)}, device_id_type=MESH,
+        )
+
+    q1 = spread(q_hbm, qt, s1q, r1q)
+    c1 = spread(c_hbm, ct, s1c, r1c)
+    own_q = pltpu.make_async_copy(q_hbm.at[:, :, cols(me)], qt.at[pl.ds(me * 16, 16)], lsem.at[2])
+    own_c = pltpu.make_async_copy(c_hbm.at[:, :, cols(me)], ct.at[pl.ds(me * 16, 16)], lsem.at[3])
+    run(1, lambda k: q1(k).start())
+    own_q.start()
+    run(1, lambda k: c1(k).start())
+    own_c.start()
+
+    @pl.when(z == hub)
+    def _():
+        def answer(k, carry):
+            pl.semaphore_signal(barrier, inc=1, device_id={"dp": zpeer(k)}, device_id_type=MESH)
+            return carry
+        lax.fori_loop(1, nz, answer, 0)
+
+    qt[pl.ds(TABLE, 16)] = jnp.zeros((16, 8, 128), jnp.bfloat16)
+    ct[pl.ds(TABLE, 16)] = jnp.zeros((16, 8, 128), jnp.bfloat16)
+    bq[pl.ds(NP * PAIR, 16)] = jnp.zeros((16, 8, 128), jnp.bfloat16)
+
+    def to_hub(buffer, send, recv):
+        return pltpu.make_async_remote_copy(
+            src_ref=buffer.at[z], dst_ref=buffer.at[z], send_sem=send, recv_sem=recv,
+            device_id={"dp": hub}, device_id_type=MESH,
+        )
+
+    def from_hub(buffer, send, recv, k):
+        return pltpu.make_async_remote_copy(
+            src_ref=buffer, dst_ref=buffer, send_sem=send, recv_sem=recv,
+            device_id={"dp": zpeer(k)}, device_id_type=MESH,
+        )
+
+    def run_z(body):
+        def step(k, carry):
+            body(k)
+            return carry
+        lax.fori_loop(1, nz, step, 0)
+
 
     def deal(table, send_buf, into, send, recv):
         def make(k):
             return pltpu.make_async_remote_copy(
                 src_ref=send_buf.at[k],
                 dst_ref=into.at[k],
-                send_sem=send.at[k],
+                send_sem=send,
                 recv_sem=recv.at[k],
                 device_id={"pack": peer(k)},
                 device_id_type=MESH,
@@ -187,11 +194,11 @@
     q2, fill_q = deal(qt, sq, qin, s2q, r2q)
     c2, fill_c = deal(ct, sc, cin, s2c, r2c)
 
-    def arrived_1(make, i):
-        make(i).wait_recv()
-
-    run(1, lambda k: q1(k).wait_recv())
+    all_q1 = total(qt.at[pl.ds(0, 16 * (NP - 1))], s1q, r1q)
+    all_q1.wait_recv()
     own_q.wait()
+
+    table_copy.wait()
 
     def send_q(k):
         fill_q(k, sq)
@@ -200,7 +207,13 @@
     run(1, send_q)
     fill_q(0, qin)
 
-    run(1, lambda k: c1(k).wait_recv())
+    @pl.when(z != hub)
+    def _():
+        pl.semaphore_wait(barrier, 1)
+        to_hub(cnt, szc, rzc).start()
+
+    all_c1 = total(ct.at[pl.ds(0, 16 * (NP - 1))], s1c, r1c)
+    all_c1.wait_recv()
     own_c.wait()
 
     def send_c(k):
@@ -215,10 +228,19 @@
     len0 = tab[1, 2 * me]
     len1 = tab[1, 2 * me + 1]
     keys0 = tab[2, 2 * me]
-    run_z(lambda k: count_arrival(k).wait_recv())
-    counts = cnt[0][:1]
-    for at in range(1, nz):
-        counts = counts + cnt[at][:1]
+    all_counts = total(cnt.at[pl.ds(0, nz - 1)], szc, rzc)
+
+    @pl.when(z == hub)
+    def _():
+        all_counts.wait_recv()
+        ctot[...] = jnp.sum(cnt[...], axis=0)
+        run_z(lambda k: from_hub(ctot, szt, rzt, k).start())
+
+    @pl.when(z != hub)
+    def _():
+        from_hub(ctot, szt, rzt, 1).wait_recv()
+
+    counts = ctot[:1]
     lane_r = lax.broadcasted_iota(jnp.int32, (1, 128), 1)
     weights = jnp.concatenate([dro_ref[...].astype(f32), jnp.zeros((1, 128 - GROUPS), f32)], axis=1)
     scales = weights / jnp.sum(weights, axis=1, keepdims=True) * (128.0 * NP * nz / counts)
@@ -259,17 +281,11 @@
         return pltpu.make_async_remote_copy(
             src_ref=sd.at[k],
             dst_ref=bq.at[pl.ds(me * PAIR, PAIR)],
-            send_sem=s3.at[k],
-            recv_sem=r3.at[k],
+            send_sem=s3,
+            recv_sem=r3,
             device_id={"pack": back(k)},
             device_id_type=MESH,
         )
-
-    def out_k(k):
-        return pltpu.make_async_copy(dks.at[k], dk_out.at[:, cols(back(k))], ksem.at[k])
-
-    def out_v(k):
-        return pltpu.make_async_copy(dvs.at[k], dv_out.at[:, cols(back(k))], vsem.at[k])
 
     def compute(k, loss):
         i = back(k)
@@ -303,27 +319,34 @@
             dq_parts.append(dot(k_t[h * 64:(h + 1) * 64], ds, nn))
             dk = dk + dot(ds, q_h, nn)
         dq = jnp.concatenate(dq_parts, axis=0).T
-        dks[k] = dk.astype(jnp.bfloat16)
-        dvs[k] = dv.astype(jnp.bfloat16)
+        dk_out[:, cols(i)] = dk.astype(jnp.bfloat16)
+        dv_out[:, cols(i)] = dv.astype(jnp.bfloat16)
         sd_block = dq[:240].reshape(PAIR, 8, 128).astype(jnp.bfloat16)
         return sd_block, loss
 
-    block, loss = compute(0, jnp.zeros((1, 256), jnp.float32))
-    bq[pl.ds(me * PAIR, PAIR)] = block
-    out_k(0).start()
-    out_v(0).start()
+    own_b = pltpu.make_async_copy(sd.at[0], bq.at[pl.ds(me * PAIR, PAIR)], lsem.at[6])
 
     def pair_step(k, loss):
-        q2(k).wait_recv()
-        c2(k).wait_recv()
+        @pl.when(k > 0)
+        def _():
+            q2(k).wait_recv()
+            c2(k).wait_recv()
+
         block, loss = compute(k, loss)
         sd[k] = block
-        d3(k).start()
-        out_k(k).start()
-        out_v(k).start()
+
+        @pl.when(k > 0)
+        def _():
+            d3(k).start()
+
+        @pl.when(k == 0)
+        def _():
+            own_b.start()
+
         return loss
 
-    loss = lax.fori_loop(1, NP, pair_step, loss)
+    loss = lax.fori_loop(0, NP, pair_step, jnp.zeros((1, 256), jnp.float32))
+    own_b.wait()
     loss = jnp.where(live_r > 0.5, loss, 0.0)
     loss0 = jnp.sum(jnp.where(place_r < 120, loss, 0.0), axis=1, keepdims=True)
     loss1 = jnp.sum(jnp.where(place_r < 120, 0.0, loss), axis=1, keepdims=True)
@@ -334,32 +357,23 @@
         return pltpu.make_async_remote_copy(
             src_ref=lpart.at[me],
             dst_ref=lpart.at[me],
-            send_sem=sl.at[k],
-            recv_sem=rl.at[k],
+            send_sem=sl,
+            recv_sem=rl,
             device_id={"pack": peer(k)},
             device_id_type=MESH,
         )
 
-    def loss_arrival(k):
-        return pltpu.make_async_remote_copy(
-            src_ref=lpart.at[back(k)],
-            dst_ref=lpart.at[back(k)],
-            send_sem=sl.at[k],
-            recv_sem=rl.at[k],
-            device_id={"pack": back(k)},
-            device_id_type=MESH,
-        )
-
     run(1, lambda k: loss_copy(k).start())
 
-    run(1, lambda k: d3(k).wait_recv())
+    all_d3 = total(bq.at[pl.ds(0, PAIR * (NP - 1))], s3, r3)
+    all_d3.wait_recv()
 
     def d4(k):
         return pltpu.make_async_remote_copy(
             src_ref=dp.at[k],
             dst_ref=dq_out.at[:, :, cols(me)],
-            send_sem=s4.at[k],
-            recv_sem=r4.at[k],
+            send_sem=s4,
+            recv_sem=r4,
             device_id={"pack": peer(k)},
             device_id_type=MESH,
         )
@@ -382,57 +396,46 @@
     fill_d(0)
     own_d.start()
 
-    run(1, lambda k: loss_arrival(k).wait_recv())
+    all_loss = total(lpart.at[pl.ds(0, NP - 1)], sl, rl)
+    all_loss.wait_recv()
     lz[z] = jnp.sum(lpart[...], axis=0)
 
-    def zloss_copy(k):
-        return pltpu.make_async_remote_copy(
-            src_ref=lz.at[z],
-            dst_ref=lz.at[z],
-            send_sem=szl.at[k],
-            recv_sem=rzl.at[k],
-            device_id={"dp": zpeer(k)},
-            device_id_type=MESH,
-        )
-
-    def zloss_arrival(k):
-        source = lax.rem(z - k + nz, nz)
-        return pltpu.make_async_remote_copy(
-            src_ref=lz.at[source],
-            dst_ref=lz.at[source],
-            send_sem=szl.at[k],
-            recv_sem=rzl.at[k],
-            device_id={"dp": source},
-            device_id_type=MESH,
-        )
-
-    run_z(lambda k: zloss_copy(k).start())
-    run_z(lambda k: zloss_arrival(k).wait_recv())
-    total = jnp.sum(lz[...], axis=0)[:1] / counts
-    loss_out[...] = total[:, :GROUPS]
-
-    def drain_z(k):
-        count_copy(k).wait_send()
-        zloss_copy(k).wait_send()
-
-    run_z(drain_z)
-
-    def drain(k):
-        loss_copy(k).wait_send()
-        q1(k).wait_send()
-        c1(k).wait_send()
-        q2(k).wait_send()
-        c2(k).wait_send()
-        d3(k).wait_send()
-        out_k(k).wait()
-        out_v(k).wait()
-        d4(k).wait_send()
-        d4(k).wait_recv()
-
-    run(1, drain)
-    out_k(0).wait()
-    out_v(0).wait()
+    all_zloss = total(lz.at[pl.ds(0, nz - 1)], szl, rzl)
+
+    @pl.when(z == hub)
+    def _():
+        all_zloss.wait_recv()
+        ltot[...] = jnp.sum(lz[...], axis=0)
+        run_z(lambda k: from_hub(ltot, szm, rzm, k).start())
+
+    @pl.when(z != hub)
+    def _():
+        to_hub(lz, szl, rzl).start()
+        from_hub(ltot, szm, rzm, 1).wait_recv()
+
+    mean_loss = ltot[:1] / counts
+    loss_out[...] = mean_loss[:, :GROUPS]
+
+
+    @pl.when(z == hub)
+    def _():
+        total(cnt.at[pl.ds(0, nz - 1)], szt, rzt).wait_send()
+        total(lz.at[pl.ds(0, nz - 1)], szm, rzm).wait_send()
+
+    @pl.when(z != hub)
+    def _():
+        to_hub(cnt, szc, rzc).wait_send()
+        to_hub(lz, szl, rzl).wait_send()
+
+    all_loss.wait_send()
+    all_q1.wait_send()
+    all_c1.wait_send()
+    total(sq.at[pl.ds(0, NP - 1)], s2q, r2q.at[0]).wait_send()
+    total(sc.at[pl.ds(0, NP - 1)], s2c, r2c.at[0]).wait_send()
+    all_d3.wait_send()
     own_d.wait()
+    total(dp.at[pl.ds(0, NP - 1)], s4, r4).wait_send()
+    total(dp.at[pl.ds(0, NP - 1)], s4, r4).wait_recv()
 
 
 def local(
@@ -447,13 +450,13 @@
     dq, dk, dv, loss = pl.pallas_call(
         kernel,
         out_shape=(
-            jax.ShapeDtypeStruct((16, 8, 4096), bf),
-            jax.ShapeDtypeStruct((256, 4096), bf),
-            jax.ShapeDtypeStruct((256, 4096), bf),
-            jax.ShapeDtypeStruct((1, GROUPS), jnp.float32),
+            pltpu.VMEM((16, 8, 4096), bf),
+            pltpu.VMEM((256, 4096), bf),
+            pltpu.VMEM((256, 4096), bf),
+            pltpu.VMEM((1, GROUPS), jnp.float32),
         ),
         in_specs=[vmem] * 6 + [hbm] * 4,
-        out_specs=(hbm, hbm, hbm, vmem),
+        out_specs=(vmem, vmem, vmem, vmem),
         scratch_shapes=[
             pltpu.VMEM((256, 4096), bf),
             pltpu.VMEM((256, 4096), bf),
@@ -466,15 +469,18 @@
             pltpu.VMEM((NP, PAIR, 8, 128), bf),
             pltpu.VMEM((NP * PAIR + 16, 8, 128), bf),
             pltpu.VMEM((NP, 16, 8, 128), bf),
-            pltpu.VMEM((NP, 256, 128), bf),
-            pltpu.VMEM((NP, 256, 128), bf),
             pltpu.VMEM((8, 128), jnp.int32),
             pltpu.SMEM((8, 128), jnp.int32),
             pltpu.VMEM((nz, 8, 128), jnp.float32),
             pltpu.VMEM((NP, 8, 128), jnp.float32),
             pltpu.VMEM((nz, 8, 128), jnp.float32),
+            pltpu.VMEM((8, 128), jnp.float32),
+            pltpu.VMEM((8, 128), jnp.float32),
             dma((8,)),
-        ] + [dma((NP,))] * 16 + [dma((nz,))] * 4,
+            dma((20,)),
+            dma((NP,)),
+            dma((NP,)),
+        ],
         compiler_params=pltpu.CompilerParams(
             collective_id=0, has_side_effects=True, vmem_limit_bytes=56 * 1024 * 1024
         ),

time: 138 us -> 126 us (0.913)
  Pallas kernels: 130 us -> 120 us
  local copies, waits for them, and re-layouts: 6.62 us -> 4.12 us
    pallas_call x1, Pallas kernels: 130 us -> 120 us  [local(): pl.pallas_call(kernel, out_shape=(pltpu.VMEM((16, 8, 4096), bf), pltpu.VM...]
    unnamed x10 -> x4, local copies, waits for them, and re-layouts: 6.62 us -> 4.12 us
where the time goes in v3:
time: 126 us; the launch traced here: 125 us
  Pallas kernels  120 us (95%)
  local copies, waits for them, and re-layouts  4.12 us (3%)
    pallas_call x1, Pallas kernels, local(): pl.pallas_call(kernel, out_shape=(pltpu.VMEM((16, 8, 4096), bf), pltpu.VM...  120 us
    unnamed x4, local copies, waits for them, and re-layouts  4.12 us

profile of v3, /device:TPU:1, one launch (start us, length us, event | category | flops | bytes accessed | tf_op | source)
XLA Modules:
  0.0 124.8 jit_solution(1720955703222930912)
XLA Ops:
  0.6 120.0 %shard_map.129 = (bf16[16,8,4096]{2,1,0:T(8,128)(2,1)S(1)}, bf16[256,4096]{1,0:T(8,128)(2,1)S(1)}, bf16[256,4096]{1,0:T(8,128)(2,1)S(1)}, f32[1,16]{1,0:T(1,128)S(1)}) custom-call(s32[1,64]{1,0:T(1,128)} %lens_e_ref.1, s32[1,64]{1,0:T(1,128)} %lens_d_ref.1, s32[1,64]{1,0:T(1,128)} %ep_ref.1, s32[1,64]{1,0:T(1,128)} %dpk_ref.1, s32[1,64]{1,0:T(1,128)} %bitcast.10, ...), custom_call_target="tpu_custom_call" | custom-call | flops 3000000000 | bytes 11000000 | tf_op jit(solution)/shard_map/pallas_call | solution.py:450
  120.6 1.0 copy.18
  121.6 0.5 copy.21
  122.1 1.3 %copy.19 = bf16[256,4096]{1,0:T(8,128)(2,1)} copy(bf16[256,4096]{1,0:T(8,128)(2,1)S(1)} %get-tuple-element.13) | data formatting | bytes 4194304
  123.4 1.3 %copy.20 = bf16[256,4096]{1,0:T(8,128)(2,1)} copy(bf16[256,4096]{1,0:T(8,128)(2,1)S(1)} %get-tuple-element.14) | data formatting | bytes 4194304

commit v4 on v3

--- a/solution.py
+++ b/solution.py
@@ -33,10 +33,13 @@
     x, y, core = me // 8, lax.rem(me // 2, 4), lax.rem(me, 2)
 
     def other(k, source):
-        j = k // 2
-        dx, dy = lax.rem(j, 4), lax.rem(j // 4 + j, 4)
-        far = lax.rem(core + k, 2)
-        sign = (2 * far - 1) if source else (1 - 2 * core)
+        j = lax.rem(k, 16)
+        d0, d1 = lax.rem(j, 4), lax.rem(j // 4 + j, 4)
+        far = lax.rem(core + k // 16, 2)
+        turn = far if source else core
+        dx = d0 + turn * (d1 - d0)
+        dy = d1 + turn * (d0 - d1)
+        sign = -1 if source else 1
         return lax.rem(x + sign * dx + 4, 4) * 8 + lax.rem(y + sign * dy + 4, 4) * 2 + far
 
     def peer(k):
@@ -67,6 +70,53 @@
     load_v.start()
     f32 = jnp.float32
     i32 = jnp.int32
+    pl.semaphore_wait(barrier, jnp.where(z == hub, NP + nz - 2, NP - 1))
+
+    @pl.when(z != hub)
+    def _():
+        pl.semaphore_signal(barrier, inc=1, device_id={"dp": hub}, device_id_type=MESH)
+
+
+    def spread(src, dst, send, recv):
+        def make(k):
+            return pltpu.make_async_remote_copy(
+                src_ref=src.at[:, :, cols(peer(k))],
+                dst_ref=dst.at[pl.ds(me * 16, 16)],
+                send_sem=send,
+                recv_sem=recv,
+                device_id={"pack": peer(k)},
+                device_id_type=MESH,
+            )
+        return make
+
+    def run(count_from, body, unroll=False):
+        def step(k, carry):
+            body(k)
+            return carry
+        lax.fori_loop(count_from, NP, step, 0, unroll=unroll)
+
+    def total(buffer, send, recv):
+        return pltpu.make_async_remote_copy(
+            src_ref=buffer, dst_ref=buffer, send_sem=send, recv_sem=recv,
+            device_id={"pack": peer(1)}, device_id_type=MESH,
+        )
+
+    q1 = spread(q_hbm, qt, s1q, r1q)
+    c1 = spread(c_hbm, ct, s1c, r1c)
+    own_q = pltpu.make_async_copy(q_hbm.at[:, :, cols(me)], qt.at[pl.ds(me * 16, 16)], lsem.at[2])
+    own_c = pltpu.make_async_copy(c_hbm.at[:, :, cols(me)], ct.at[pl.ds(me * 16, 16)], lsem.at[3])
+    run(1, lambda k: q1(k).start())
+    own_q.start()
+    run(1, lambda k: c1(k).start())
+    own_c.start()
+
+    @pl.when(z == hub)
+    def _():
+        def answer(k, carry):
+            pl.semaphore_signal(barrier, inc=1, device_id={"dp": zpeer(k)}, device_id_type=MESH)
+            return carry
+        lax.fori_loop(1, nz, answer, 0)
+
     lens_e_r = lens_e_ref[...]
     lens_d_r = lens_d_ref[...]
     ep_r = ep_ref[...]
@@ -102,53 +152,6 @@
     tab_v[...] = wide.T[:8]
     table_copy = pltpu.make_async_copy(tab_v, tab, lsem.at[5])
     table_copy.start()
-    pl.semaphore_wait(barrier, jnp.where(z == hub, NP + nz - 2, NP - 1))
-
-    @pl.when(z != hub)
-    def _():
-        pl.semaphore_signal(barrier, inc=1, device_id={"dp": hub}, device_id_type=MESH)
-
-
-    def spread(src, dst, send, recv):
-        def make(k):
-            return pltpu.make_async_remote_copy(
-                src_ref=src.at[:, :, cols(peer(k))],
-                dst_ref=dst.at[pl.ds(me * 16, 16)],
-                send_sem=send,
-                recv_sem=recv,
-                device_id={"pack": peer(k)},
-                device_id_type=MESH,
-            )
-        return make
-
-    def run(count_from, body, unroll=False):
-        def step(k, carry):
-            body(k)
-            return carry
-        lax.fori_loop(count_from, NP, step, 0, unroll=unroll)
-
-    def total(buffer, send, recv):
-        return pltpu.make_async_remote_copy(
-            src_ref=buffer, dst_ref=buffer, send_sem=send, recv_sem=recv,
-            device_id={"pack": peer(1)}, device_id_type=MESH,
-        )
-
-    q1 = spread(q_hbm, qt, s1q, r1q)
-    c1 = spread(c_hbm, ct, s1c, r1c)
-    own_q = pltpu.make_async_copy(q_hbm.at[:, :, cols(me)], qt.at[pl.ds(me * 16, 16)], lsem.at[2])
-    own_c = pltpu.make_async_copy(c_hbm.at[:, :, cols(me)], ct.at[pl.ds(me * 16, 16)], lsem.at[3])
-    run(1, lambda k: q1(k).start())
-    own_q.start()
-    run(1, lambda k: c1(k).start())
-    own_c.start()
-
-    @pl.when(z == hub)
-    def _():
-        def answer(k, carry):
-            pl.semaphore_signal(barrier, inc=1, device_id={"dp": zpeer(k)}, device_id_type=MESH)
-            return carry
-        lax.fori_loop(1, nz, answer, 0)
-
     qt[pl.ds(TABLE, 16)] = jnp.zeros((16, 8, 128), jnp.bfloat16)
     ct[pl.ds(TABLE, 16)] = jnp.zeros((16, 8, 128), jnp.bfloat16)
     bq[pl.ds(NP * PAIR, 16)] = jnp.zeros((16, 8, 128), jnp.bfloat16)

time: 126 us -> 122 us (0.968)
  Pallas kernels: 120 us -> 117 us
    pallas_call x1, Pallas kernels: 120 us -> 117 us  [local(): pl.pallas_call(kernel, out_shape=(pltpu.VMEM((16, 8, 4096), bf), pltpu.VM...]
where the time goes in v4:
time: 122 us
  Pallas kernels  117 us (96%)
  local copies, waits for them, and re-layouts  4.12 us (3%)
    pallas_call x1, Pallas kernels, local(): pl.pallas_call(kernel, out_shape=(pltpu.VMEM((16, 8, 4096), bf), pltpu.VM...  117 us
    unnamed x4, local copies, waits for them, and re-layouts  4.12 us

profile of v4, /device:TPU:1, one launch (start us, length us, event | category | flops | bytes accessed | tf_op | source)
XLA Modules:
  0.0 121.9 jit_solution(15699655429001530791)
XLA Ops:
  0.6 117.2 %shard_map.129 = (bf16[16,8,4096]{2,1,0:T(8,128)(2,1)S(1)}, bf16[256,4096]{1,0:T(8,128)(2,1)S(1)}, bf16[256,4096]{1,0:T(8,128)(2,1)S(1)}, f32[1,16]{1,0:T(1,128)S(1)}) custom-call(s32[1,64]{1,0:T(1,128)} %lens_e_ref.1, s32[1,64]{1,0:T(1,128)} %lens_d_ref.1, s32[1,64]{1,0:T(1,128)} %ep_ref.1, s32[1,64]{1,0:T(1,128)} %dpk_ref.1, s32[1,64]{1,0:T(1,128)} %bitcast.10, ...), custom_call_target="tpu_custom_call" | custom-call | flops 3000000000 | bytes 11000000 | tf_op jit(solution)/shard_map/pallas_call | solution.py:453
  117.8 1.0 copy.18
  118.8 0.5 copy.21
  119.3 1.3 %copy.19 = bf16[256,4096]{1,0:T(8,128)(2,1)} copy(bf16[256,4096]{1,0:T(8,128)(2,1)S(1)} %get-tuple-element.13) | data formatting | bytes 4194304
  120.6 1.3 %copy.20 = bf16[256,4096]{1,0:T(8,128)(2,1)} copy(bf16[256,4096]{1,0:T(8,128)(2,1)S(1)} %get-tuple-element.14) | data formatting | bytes 4194304

commit v5 on v4

--- a/solution.py
+++ b/solution.py
@@ -37,10 +37,10 @@
         d0, d1 = lax.rem(j, 4), lax.rem(j // 4 + j, 4)
         far = lax.rem(core + k // 16, 2)
         turn = far if source else core
-        dx = d0 + turn * (d1 - d0)
+        dx = d0 + turn * (4 - d1 - d0)
         dy = d1 + turn * (d0 - d1)
         sign = -1 if source else 1
-        return lax.rem(x + sign * dx + 4, 4) * 8 + lax.rem(y + sign * dy + 4, 4) * 2 + far
+        return lax.rem(x + sign * dx + 8, 4) * 8 + lax.rem(y + sign * dy + 8, 4) * 2 + far
 
     def peer(k):
         return other(k, False)

time: 122 us -> 122 us (level)
  no operation moved by 1% of the time
where the time goes in v5:
time: 122 us; the launch traced here: 121 us
  Pallas kernels  116 us (95%)
  local copies, waits for them, and re-layouts  4.12 us (3%)
    pallas_call x1, Pallas kernels, local(): pl.pallas_call(kernel, out_shape=(pltpu.VMEM((16, 8, 4096), bf), pltpu.VM...  116 us
    unnamed x4, local copies, waits for them, and re-layouts  4.12 us

profile of v5, /device:TPU:1, one launch (start us, length us, event | category | flops | bytes accessed | tf_op | source)
XLA Modules:
  0.0 121.0 jit_solution(9687345340532080932)
XLA Ops:
  0.6 116.2 %shard_map.129 = (bf16[16,8,4096]{2,1,0:T(8,128)(2,1)S(1)}, bf16[256,4096]{1,0:T(8,128)(2,1)S(1)}, bf16[256,4096]{1,0:T(8,128)(2,1)S(1)}, f32[1,16]{1,0:T(1,128)S(1)}) custom-call(s32[1,64]{1,0:T(1,128)} %lens_e_ref.1, s32[1,64]{1,0:T(1,128)} %lens_d_ref.1, s32[1,64]{1,0:T(1,128)} %ep_ref.1, s32[1,64]{1,0:T(1,128)} %dpk_ref.1, s32[1,64]{1,0:T(1,128)} %bitcast.10, ...), custom_call_target="tpu_custom_call" | custom-call | flops 3000000000 | bytes 11000000 | tf_op jit(solution)/shard_map/pallas_call | solution.py:453
  116.8 1.0 copy.18
  117.8 0.5 copy.21
  118.3 1.3 %copy.19 = bf16[256,4096]{1,0:T(8,128)(2,1)} copy(bf16[256,4096]{1,0:T(8,128)(2,1)S(1)} %get-tuple-element.13) | data formatting | bytes 4194304
  119.6 1.3 %copy.20 = bf16[256,4096]{1,0:T(8,128)(2,1)} copy(bf16[256,4096]{1,0:T(8,128)(2,1)S(1)} %get-tuple-element.14) | data formatting | bytes 4194304
